TPU v7x, 256 devices: a whole 4x4x8 slice. The times are simulated.
256 devices in a mesh: seq: 64 (over x, z, y_lo), ch: 4 (over y_hi, core).
Axes of the slice: x: 4, y: 4 (y_hi: 2, y_lo: 2; y = y_hi * 2 + y_lo), z: 8, core: 2. Of those that a mesh axis runs over, the one named last changes fastest.
Arguments:
- grad_output: bfloat16 [8192, 16, 512], P('seq', 'ch'), may hold values from -6 to 6
- query_act: bfloat16 [8192, 16, 512], P('seq', 'ch'), may hold values from -6 to 6
- key_act: bfloat16 [8192, 16, 512], P('seq', 'ch'), may hold values from -6 to 6
- value_act: bfloat16 [8192, 16, 512], P('seq', 'ch'), may hold values from -6 to 6
- long_filter: bfloat16 [8192, 512], P('seq'), may hold values from -0.0625 to 0.0625
Outputs:
- input_grad: bfloat16 [3, 8192, 16, 512], P(None, 'seq', 'ch')
- filter_grad: float32 [8192, 512], P('seq', 'ch')
All inputs are finite; a program needn't handle non-finite values.
Results may differ from a plain program's by a relative error of at most 0.0049.
Values may be sent and summed in bfloat16 or wider, within the bound.
A program may use at most 128 MiB of HBM per device.

v0:
```python
import math

import jax
import jax.numpy as jnp
from jax import lax
from jax.sharding import PartitionSpec as P

MEMBERS = 16


highest = lax.Precision.HIGHEST


def phases(first_index, second_index, period, direction):
    product = first_index[:, None] * second_index[None, :] % period
    angles = product.astype(jnp.float32) * (2.0 * math.pi / period)
    return (jnp.cos(angles), direction * jnp.sin(angles))


def times_complex(left_real, left_imaginary, right_real, right_imaginary):
    return (
        left_real * right_real - left_imaginary * right_imaginary,
        left_real * right_imaginary + left_imaginary * right_real,
    )


def across_forward(values, seq_count):
    cosine, sine_part = phases(
        jnp.arange(2 * seq_count, dtype=jnp.int32),
        jnp.arange(seq_count, dtype=jnp.int32),
        2 * seq_count,
        -1.0,
    )
    real_part = jnp.einsum("an,jnxc->jaxc", cosine, values, precision=highest)
    imag_part = jnp.einsum("an,jnxc->jaxc", sine_part, values, precision=highest)
    return (real_part, imag_part)


def across_inverse(real_part, imag_part, seq_count, padded):
    cosine, sine_part = phases(
        jnp.arange(seq_count, dtype=jnp.int32),
        jnp.arange(2 * seq_count, dtype=jnp.int32),
        2 * seq_count,
        1.0,
    )
    summed = jnp.einsum("na,jaxc->jnxc", cosine, real_part, precision=highest)
    summed = summed - jnp.einsum("na,jaxc->jnxc", sine_part, imag_part, precision=highest)
    return summed * (1.0 / padded)


def within(real_part, imag_part, direction):
    length = real_part.shape[2]
    counter = jnp.arange(length, dtype=jnp.int32)
    cosine, sine_part = phases(counter, counter, length, direction)

    def contract(matrix, values):
        return jnp.einsum("bn,janc->jabc", matrix, values, precision=highest)

    return (
        contract(cosine, real_part) - contract(sine_part, imag_part),
        contract(cosine, imag_part) + contract(sine_part, real_part),
    )


def twiddle(real_part, imag_part, freq_index, row_index, padded, direction):
    cosine, sine_part = phases(freq_index, row_index, padded, direction)
    return times_complex(
        real_part, imag_part, cosine[None, :, :, None], sine_part[None, :, :, None]
    )


def spectral_products(real_part, imag_part, members, chan_axis):
    item_count = 2 * members + 1

    def split_items(part):
        moved_part = jnp.moveaxis(part, chan_axis, -1)
        leading = moved_part.shape[:-1]
        return moved_part.reshape(leading + (item_count, moved_part.shape[-1] // item_count))

    def join_items(conv_part, input_part, lag_part):
        merged = jnp.concatenate([conv_part, input_part, lag_part], axis=-2)
        merged = merged.reshape(merged.shape[:-2] + (merged.shape[-2] * merged.shape[-1],))
        return jnp.moveaxis(merged, -1, chan_axis)

    real_split = split_items(real_part)
    imag_split = split_items(imag_part)
    gate_real = real_split[..., :members, :]
    gate_imaginary = imag_split[..., :members, :]
    mixed_real = real_split[..., members : 2 * members, :]
    mixed_imaginary = imag_split[..., members : 2 * members, :]
    filter_real = real_split[..., 2 * members :, :]
    filter_imaginary = imag_split[..., 2 * members :, :]
    conv_real = filter_real * mixed_real - filter_imaginary * mixed_imaginary
    conv_imaginary = filter_real * mixed_imaginary + filter_imaginary * mixed_real
    input_real = filter_real * gate_real + filter_imaginary * gate_imaginary
    input_imaginary = filter_real * gate_imaginary - filter_imaginary * gate_real
    lag_real = jnp.sum(
        gate_real * mixed_real + gate_imaginary * mixed_imaginary, axis=-2, keepdims=True
    )
    lag_imaginary = jnp.sum(
        gate_imaginary * mixed_real - gate_real * mixed_imaginary, axis=-2, keepdims=True
    )
    return (
        join_items(conv_real, input_real, lag_real),
        join_items(conv_imaginary, input_imaginary, lag_imaginary),
    )


def local(grad_output, query_act, key_act, value_act, long_filter):
    block_len = grad_output.shape[0]
    members = grad_output.shape[1]
    groups = grad_output.shape[2]
    item_count = 2 * members + 1
    seq_count = lax.axis_size("seq")
    padded = 2 * block_len * seq_count
    gated_grad = (grad_output.astype(jnp.float32) * query_act.astype(jnp.float32)).astype(
        jnp.bfloat16
    )
    mixed_input = (key_act.astype(jnp.float32) * value_act.astype(jnp.float32)).astype(jnp.bfloat16)
    stacked = jnp.concatenate([gated_grad, mixed_input, long_filter[:, None, :]], axis=1)
    freq_all = jnp.arange(2 * seq_count, dtype=jnp.int32)
    rows_all = jnp.arange(block_len, dtype=jnp.int32)
    piece_len = block_len // seq_count
    width = item_count * groups
    columns = lax.all_to_all(
        stacked.reshape(1, seq_count, piece_len, width),
        "seq",
        split_axis=1,
        concat_axis=1,
        tiled=True,
    )
    own_rows = lax.axis_index("seq") * piece_len + jnp.arange(piece_len, dtype=jnp.int32)
    real_part, imag_part = across_forward(columns.astype(jnp.float32), seq_count)
    real_part, imag_part = twiddle(real_part, imag_part, freq_all, own_rows, padded, -1.0)
    real_part, imag_part = (
        lax.all_to_all(real_part, "seq", split_axis=1, concat_axis=2, tiled=True),
        lax.all_to_all(imag_part, "seq", split_axis=1, concat_axis=2, tiled=True),
    )
    real_part, imag_part = within(real_part, imag_part, -1.0)
    real_part, imag_part = spectral_products(real_part, imag_part, members, 3)
    real_part, imag_part = within(real_part, imag_part, 1.0)
    own_freq = lax.axis_index("seq") * 2 + jnp.arange(2, dtype=jnp.int32)
    real_part, imag_part = twiddle(real_part, imag_part, own_freq, rows_all, padded, 1.0)
    real_part, imag_part = (
        lax.all_to_all(real_part, "seq", split_axis=2, concat_axis=1, tiled=True),
        lax.all_to_all(imag_part, "seq", split_axis=2, concat_axis=1, tiled=True),
    )
    result = across_inverse(real_part, imag_part, seq_count, padded)
    returned = lax.all_to_all(result, "seq", split_axis=1, concat_axis=2, tiled=True).reshape(
        block_len, item_count, groups
    )
    conv_out = returned[:, :members]
    mixed_grad = returned[:, members : 2 * members]
    lag_grad = returned[:, 2 * members]
    query_grad = (grad_output.astype(jnp.float32) * conv_out).astype(jnp.bfloat16)
    key_grad = (mixed_grad * value_act.astype(jnp.float32)).astype(jnp.bfloat16)
    value_grad = (mixed_grad * key_act.astype(jnp.float32)).astype(jnp.bfloat16)
    input_grad = jnp.stack([query_grad, key_grad, value_grad])
    lag_term = lag_grad * (1.0 / math.sqrt(MEMBERS * (padded // 2)))
    filter_grad = lax.psum_scatter(lag_term, "ch", scatter_dimension=1, tiled=True)
    return (input_grad, filter_grad)


def solution(mesh):
    in_specs = (
        P("seq", "ch", None),
        P("seq", "ch", None),
        P("seq", "ch", None),
        P("seq", "ch", None),
        P("seq", None),
    )
    out_specs = (P(None, "seq", "ch", None), P("seq", "ch"))
    return jax.shard_map(local, mesh=mesh, in_specs=in_specs, out_specs=out_specs, check_vma=False)
```

profile of v0, /device:TPU:1, one launch (start us, length us, event | category | flops | bytes accessed | tf_op | source)
XLA Modules:
  0.0 712.8 jit_solution(1896290871949820557)
XLA Ops:
  13.1 13.5 %all-to-all-start = ((bf16[1,64,2,4608]{3,2,0,1:T(2,128)(2,1)}), bf16[1,64,2,4608]{3,2,0,1:T(2,128)(2,1)S(1)}, u32[]{:S(2)}, u32[]{:S(2)}) async-start(bf16[1,64,2,4608]{3,2,0,1:T(2,128)(2,1)} %bitcast.1), calls=%async_computation | async-start | bytes 2359296 | tf_op jit(solution)/shard_map/all_to_all | solution.py:125
  26.7 29.9 %all-to-all-done = bf16[1,64,2,4608]{3,2,0,1:T(2,128)(2,1)S(1)} async-done(((bf16[1,64,2,4608]{3,2,0,1:T(2,128)(2,1)}), bf16[1,64,2,4608]{3,2,0,1:T(2,128)(2,1)S(1)}, u32[]{:S(2)}, u32[]{:S(2)}) %all-to-all-start) | async-done | bytes 1179680 | tf_op jit(solution)/shard_map/all_to_all | solution.py:125
  59.3 5.6 multiply_subtract_fusion
  64.9 8.2 %copy.48 = f32[1,128,2,4608]{3,2,0,1:T(2,128)} copy(f32[1,128,2,4608]{1,3,2,0:T(8,128)} %get-tuple-element.12) | data formatting | bytes 9437184 | tf_op jit(solution)/shard_map/sub | solution.py:22
  73.1 7.4 %all-to-all-start.1 = ((f32[1,128,2,4608]{3,2,0,1:T(2,128)}), f32[1,128,2,4608]{3,2,0,1:T(2,128)}, u32[]{:S(2)}, u32[]{:S(2)}) async-start(f32[1,128,2,4608]{3,2,0,1:T(2,128)} %copy.48), calls=%async_computation.1 | async-start | bytes 9437184 | tf_op jit(solution)/shard_map/all_to_all | solution.py:136
  80.5 8.2 %copy.51 = f32[1,128,2,4608]{3,2,0,1:T(2,128)} copy(f32[1,128,2,4608]{1,3,2,0:T(8,128)} %get-tuple-element.13) | data formatting | bytes 9437184 | tf_op jit(solution)/shard_map/add | solution.py:23
  88.7 96.3 %all-to-all-done.1 = f32[1,128,2,4608]{3,2,0,1:T(2,128)} async-done(((f32[1,128,2,4608]{3,2,0,1:T(2,128)}), f32[1,128,2,4608]{3,2,0,1:T(2,128)}, u32[]{:S(2)}, u32[]{:S(2)}) %all-to-all-start.1) | async-done | bytes 4718624 | tf_op jit(solution)/shard_map/all_to_all | solution.py:136
  185.0 9.1 %all-to-all-start.2 = ((f32[1,128,2,4608]{3,2,0,1:T(2,128)}), f32[1,128,2,4608]{3,2,0,1:T(2,128)}, u32[]{:S(2)}, u32[]{:S(2)}) async-start(f32[1,128,2,4608]{3,2,0,1:T(2,128)} %copy.51), calls=%async_computation.2 | async-start | bytes 9437184 | tf_op jit(solution)/shard_map/all_to_all | solution.py:137
  194.2 6.9 copy.49
  201.1 8.1 %copy.50 = f32[2,128,4608]{1,2,0:T(8,128)} copy(f32[2,128,4608]{2,0,1:T(2,128)} %bitcast.129) | data formatting | bytes 9437184 | tf_op jit(solution)/shard_map/reshape.12
  209.2 7.6 %fusion.29 = f32[2,4608,128]{2,1,0:T(8,128)} fusion(f32[2,128,4608]{1,2,0:T(8,128)} %copy.50), kind=kOutput, calls=%fused_computation.62 | convolution fusion | flops 1812168704 | bytes 9437184 | tf_op jit(solution)/shard_map/bn,janc->jabc/dot_general | solution.py:57
  216.8 81.7 %all-to-all-done.2 = f32[1,128,2,4608]{3,2,0,1:T(2,128)} async-done(((f32[1,128,2,4608]{3,2,0,1:T(2,128)}), f32[1,128,2,4608]{3,2,0,1:T(2,128)}, u32[]{:S(2)}, u32[]{:S(2)}) %all-to-all-start.2) | async-done | bytes 4718624 | tf_op jit(solution)/shard_map/all_to_all | solution.py:137
  298.5 6.9 copy.52
  305.5 8.1 %copy.53 = f32[2,128,4608]{1,2,0:T(8,128)} copy(f32[2,128,4608]{2,0,1:T(2,128)} %bitcast.130) | data formatting | bytes 9437184 | tf_op jit(solution)/shard_map/reshape.18
  313.6 6.7 fusion.27
  331.0 4.3 fusion.25
  340.0 4.6 fusion
  344.6 7.6 %add_bitcast_fusion = (f32[1,2,128,4608]{2,3,1,0:T(8,128)}, f32[1,2,128,4608]{2,3,1,0:T(8,128)}) fusion(f32[1,2,4608,128]{3,2,1,0:T(8,128)S(1)} %fusion, f32[2,128]{1,0:T(2,128)S(1)} %get-tuple-element.20, f32[2,128]{1,0:T(2,128)S(1)} %get-tuple-element.19, f32[2,4608,128]{2,1,0:T(8,128)S(1)} %fusion.23, f32[2,128,4608]{1,2,0:T(8,128)S(1)} %bitcast.128), kind=kOutput, calls=%fused_computation.13 | convolution fusion | flops 1820426240 | bytes 23595008 | tf_op jit(solution)/shard_map/bn,janc->jabc/dot_general | solution.py:57
  352.1 8.2 %copy.56 = f32[1,2,128,4608]{3,1,0,2:T(2,128)} copy(f32[1,2,128,4608]{2,3,1,0:T(8,128)} %get-tuple-element.11) | data formatting | bytes 9437184 | tf_op jit(solution)/shard_map/sub | solution.py:22
  360.3 8.9 %all-to-all-start.3 = ((f32[1,2,128,4608]{3,1,0,2:T(2,128)}), f32[1,2,128,4608]{3,1,0,2:T(2,128)}, u32[]{:S(2)}, u32[]{:S(2)}) async-start(f32[1,2,128,4608]{3,1,0,2:T(2,128)} %copy.56), calls=%async_computation.3 | async-start | bytes 9437184 | tf_op jit(solution)/shard_map/all_to_all | solution.py:145
  369.2 8.1 %copy.58 = f32[1,2,128,4608]{3,1,0,2:T(2,128)} copy(f32[1,2,128,4608]{2,3,1,0:T(8,128)} %get-tuple-element.10) | data formatting | bytes 9437184 | tf_op jit(solution)/shard_map/add | solution.py:23
  377.3 96.5 %all-to-all-done.3 = f32[1,2,128,4608]{3,1,0,2:T(2,128)} async-done(((f32[1,2,128,4608]{3,1,0,2:T(2,128)}), f32[1,2,128,4608]{3,1,0,2:T(2,128)}, u32[]{:S(2)}, u32[]{:S(2)}) %all-to-all-start.3) | async-done | bytes 4718624 | tf_op jit(solution)/shard_map/all_to_all | solution.py:145
  473.9 8.7 %all-to-all-start.4 = ((f32[1,2,128,4608]{3,1,0,2:T(2,128)}), f32[1,2,128,4608]{3,1,0,2:T(2,128)}, u32[]{:S(2)}, u32[]{:S(2)}) async-start(f32[1,2,128,4608]{3,1,0,2:T(2,128)} %copy.58), calls=%async_computation.4 | async-start | bytes 9437184 | tf_op jit(solution)/shard_map/all_to_all | solution.py:146
  482.6 4.8 copy.57
  487.4 6.5 reshape.226
  493.9 4.8 fusion.43
  498.7 88.5 %all-to-all-done.4 = f32[1,2,128,4608]{3,1,0,2:T(2,128)} async-done(((f32[1,2,128,4608]{3,1,0,2:T(2,128)}), f32[1,2,128,4608]{3,1,0,2:T(2,128)}, u32[]{:S(2)}, u32[]{:S(2)}) %all-to-all-start.4) | async-done | bytes 4718624 | tf_op jit(solution)/shard_map/all_to_all | solution.py:146
  587.2 4.8 copy.59
  592.0 6.6 reshape.227
  598.6 4.9 fusion.3
  605.3 63.5 %all_to_all.74 = f32[1,64,2,4608]{3,2,0,1:T(2,128)S(1)} all-to-all(f32[1,64,2,4608]{3,2,0,1:T(2,128)S(1)} %copy.60), channel_id=1, replica_groups=mesh['seq'=64,'ch'=4] {'seq'}, dimensions={1} | all-to-all | bytes 4718592 | tf_op jit(solution)/shard_map/all_to_all | solution.py:149
  680.3 25.3 %reduce-scatter.2.cloned.1.call-done = f32[128,128]{1,0:T(8,128)} async-done(((f32[128,512]{1,0:T(8,128)}), f32[128,128]{1,0:T(8,128)}) %reduce-scatter.2.cloned.1.call-update) | async-done | bytes 65552 | tf_op jit(solution)/shard_map/reduce_scatter | solution.py:160
  (37 shorter events, 37.4 us)
Async XLA Ops:
  13.1 43.6 %all-to-all-start = ((bf16[1,64,2,4608]{3,2,0,1:T(2,128)(2,1)}), bf16[1,64,2,4608]{3,2,0,1:T(2,128)(2,1)S(1)}, u32[]{:S(2)}, u32[]{:S(2)}) async-start(bf16[1,64,2,4608]{3,2,0,1:T(2,128)(2,1)} %bitcast.1), calls=%async_computation | async-start | bytes 2359296 | tf_op jit(solution)/shard_map/all_to_all | solution.py:125
  73.1 111.9 %all-to-all-start.1 = ((f32[1,128,2,4608]{3,2,0,1:T(2,128)}), f32[1,128,2,4608]{3,2,0,1:T(2,128)}, u32[]{:S(2)}, u32[]{:S(2)}) async-start(f32[1,128,2,4608]{3,2,0,1:T(2,128)} %copy.48), calls=%async_computation.1 | async-start | bytes 9437184 | tf_op jit(solution)/shard_map/all_to_all | solution.py:136
  185.0 113.5 %all-to-all-start.2 = ((f32[1,128,2,4608]{3,2,0,1:T(2,128)}), f32[1,128,2,4608]{3,2,0,1:T(2,128)}, u32[]{:S(2)}, u32[]{:S(2)}) async-start(f32[1,128,2,4608]{3,2,0,1:T(2,128)} %copy.51), calls=%async_computation.2 | async-start | bytes 9437184 | tf_op jit(solution)/shard_map/all_to_all | solution.py:137
  313.6 6.7 copy-start
  313.6 6.8 copy-start.1
  313.6 10.9 %slice-start = ((s8[4718592]{0:T(1024)(128)(4,1)}), s8[4194304]{0:T(1024)(128)(4,1)S(1)}, s32[]{:S(2)}) async-start(s8[4718592]{0:T(1024)(128)(4,1)} %bitcast.123), calls=%async_computation.8 | async-start | bytes 8388608
  320.3 4.1 slice-start.1
  360.3 113.6 %all-to-all-start.3 = ((f32[1,2,128,4608]{3,1,0,2:T(2,128)}), f32[1,2,128,4608]{3,1,0,2:T(2,128)}, u32[]{:S(2)}, u32[]{:S(2)}) async-start(f32[1,2,128,4608]{3,1,0,2:T(2,128)} %copy.56), calls=%async_computation.3 | async-start | bytes 9437184 | tf_op jit(solution)/shard_map/all_to_all | solution.py:145
  473.9 113.3 %all-to-all-start.4 = ((f32[1,2,128,4608]{3,1,0,2:T(2,128)}), f32[1,2,128,4608]{3,1,0,2:T(2,128)}, u32[]{:S(2)}, u32[]{:S(2)}) async-start(f32[1,2,128,4608]{3,1,0,2:T(2,128)} %copy.58), calls=%async_computation.4 | async-start | bytes 9437184 | tf_op jit(solution)/shard_map/all_to_all | solution.py:146
  482.5 223.1 %reduce-scatter.2.cloned.1.call-start = ((), (), s32[]{:S(2)}) async-start(), calls=%async_computation.7 | async-start | bytes 327680 | tf_op jit(solution)/shard_map/reduce_scatter | solution.py:160
  668.8 6.0 copy-start.2
  668.8 6.0 copy-start.3
Sparse Core Ops, SparseCore 0:
  674.9 30.6 reduce-scatter.1
where the time goes:
time: 722 us; the launch traced here: 713 us
  waiting for transfers between devices  418 us (58%)
  local copies, waits for them, and re-layouts  94 us (13%)
  blocking collectives  63.5 us (9%)
  matrix products  61.2 us (8%)
  starting transfers between devices  47.5 us (7%)
  between operations  14.7 us (2%)
  other arithmetic  13.6 us (2%)
    all_to_all x1, waiting for transfers between devices, local(): lax.all_to_all(real_part, 'seq', split_axis=2, concat_axis=1, tiled=True)  96.5 us
    all_to_all x1, waiting for transfers between devices, local(): lax.all_to_all(real_part, 'seq', split_axis=1, concat_axis=2, tiled=True)  96.3 us
    all_to_all x1, waiting for transfers between devices, local(): lax.all_to_all(imag_part, 'seq', split_axis=2, concat_axis=1, tiled=True)  88.5 us
    all_to_all x1, waiting for transfers between devices, local(): lax.all_to_all(imag_part, 'seq', split_axis=1, concat_axis=2, tiled=True)  81.7 us
    all_to_all x1, blocking collectives, local(): lax.all_to_all(result, 'seq', split_axis=1, concat_axis=2, tiled=True)  63.5 us
    dot_general x8, matrix products, contract(): return jnp.einsum('bn,janc->jabc', matrix, values, precision=highest)  43.2 us
    all_to_all x1, waiting for transfers between devices, local(): lax.all_to_all(stacked.reshape(1, seq_count, piece_len, width), 'seq', sp...  29.9 us
    another operation x4, local copies, waits for them, and re-layouts  29.3 us
  transfers between devices with their start and end apart: 6, of which 6 were waited for; matrix products, arithmetic and copies ran while one was open for 9% of the time, Pallas kernels for 0%

commit v1 on v0

v1 whole, which is shorter than its diff:
```python
import math

import jax
import jax.numpy as jnp
from jax import lax
from jax.experimental import pallas as pl
from jax.experimental.pallas import tpu as pltpu
from jax.sharding import PartitionSpec as P

F32 = jnp.float32
BF16 = jnp.bfloat16

SEQ = 64
CH = 4
DEVICES = SEQ * CH
BLOCK = 128
MEMBERS = 16
OWN = 4
GROUPS = 512
TILES = GROUPS // 128
PAIR = 2 * BLOCK
STEPS = SEQ // 2
ROWS = STEPS * MEMBERS
SCALE = 1.0 / math.sqrt(MEMBERS * SEQ * BLOCK)


def dot_rows(left, right):
    return lax.dot_general(
        left, right, (((1,), (1,)), ((), ())), preferred_element_type=F32
    )


def dot(left, right):
    return jnp.dot(left, right, preferred_element_type=F32)


def products(left, right, rows):
    def body(k, carry):
        at = pl.ds(pl.multiple_of(16 * k, 16), 16)
        value = (left[at].astype(F32) * right[at].astype(F32)).astype(BF16).astype(F32)
        value = value.reshape(64, GROUPS)
        for tile in range(TILES):
            rows[tile, pl.ds(pl.multiple_of(64 * k, 64), 64), :] = value[
                :, 128 * tile : 128 * tile + 128
            ]
        return carry

    lax.fori_loop(0, BLOCK // 16, body, 0)


def spread(mixed_rows, gated_rows, tile, turned, send):
    for arr, rows in enumerate((mixed_rows, gated_rows)):
        for m in range(OWN):
            part = rows.at[tile][pl.ds(m, BLOCK, stride=OWN), :]
            turned[pl.ds(arr * OWN + m, 128, stride=8), :] = part.T
    low = 2 * (tile % 2)
    send[tile // 2, low : low + 2] = turned[...].reshape(2, SEQ, 8, BLOCK).astype(BF16)


def collect(recv, tile, turned, conv_rows, back_rows):
    low = 2 * (tile % 2)
    turned[...] = recv[tile // 2, low : low + 2].astype(F32).reshape(1024, BLOCK)
    for arr, rows in enumerate((conv_rows, back_rows)):
        for m in range(OWN):
            part = turned[pl.ds(arr * OWN + m, 128, stride=8), :]
            rows.at[tile][pl.ds(m, BLOCK, stride=OWN), :] = part.T


def gradients(tile, conv_rows, back_rows, grad, key, value, out):
    lanes = pl.ds(128 * tile, 128)

    def body(k, carry):
        at = pl.ds(pl.multiple_of(16 * k, 16), 16)
        rows = pl.ds(pl.multiple_of(64 * k, 64), 64)
        conv = conv_rows[tile, rows, :].reshape(16, OWN, 128)
        back = back_rows[tile, rows, :].reshape(16, OWN, 128)
        out[0, at, :, lanes] = (grad[at, :, lanes].astype(F32) * conv).astype(BF16)
        out[1, at, :, lanes] = (back * value[at, :, lanes].astype(F32)).astype(BF16)
        out[2, at, :, lanes] = (back * key[at, :, lanes].astype(F32)).astype(BF16)
        return carry

    lax.fori_loop(0, BLOCK // 16, body, 0)


def toeplitz(taps, half, strip):
    strip[half, :, 0:128] = jnp.zeros((128, 128), BF16)

    def body(t, carry):
        now = taps[half, pl.ds(t, 1), :]
        before = taps[half, pl.ds(jnp.maximum(t - 1, 0), 1), :] * jnp.where(t > 0, 1.0, 0.0)
        both = jnp.broadcast_to(jnp.concatenate([before, now], axis=1), (128, 256))
        skewed = pltpu.roll(both, 0, 1, stride=1, stride_axis=0)
        at = pl.ds(pl.multiple_of(128 * (t + 1), 128), 128)
        strip[half, :, at] = skewed[:, 128:].astype(BF16)
        return carry

    lax.fori_loop(0, SEQ, body, 0, unroll=8)


def unpack(recv, half, mixed, gated):
    def body(j, carry):
        rows = pl.ds(pl.multiple_of(MEMBERS * j, MEMBERS), MEMBERS)
        for h in range(2):
            inputs, gates = [], []
            for c in (0, 2):
                low = recv[half, c, 2 * j + h].astype(F32)
                high = recv[half, c + 1, 2 * j + h].astype(F32)
                inputs.append(jnp.concatenate([low[:OWN], high[:OWN]], axis=0))
                gates.append(jnp.concatenate([low[OWN:], high[OWN:]], axis=0))
            lanes = slice(128 * h, 128 * h + 128)
            mixed[rows, lanes] = jnp.concatenate(inputs, axis=0).astype(BF16)
            gated[rows, lanes] = jnp.concatenate(gates, axis=0).astype(BF16)
        return carry

    lax.fori_loop(0, STEPS, body, 0, unroll=4)


def pack(conv, back, half, send):
    def body(i, carry):
        for h in range(2):
            lanes = slice(128 * h, 128 * h + 128)
            for c in (0, 2):
                rows = pl.ds(pl.multiple_of(MEMBERS * i + OWN * c, 8), 8)
                y = conv[rows, lanes]
                m = back[rows, lanes]
                send[half, c, 2 * i + h] = jnp.concatenate([y[:OWN], m[:OWN]], axis=0).astype(BF16)
                send[half, c + 1, 2 * i + h] = jnp.concatenate([y[OWN:], m[OWN:]], axis=0).astype(BF16)
        return carry

    lax.fori_loop(0, STEPS, body, 0, unroll=4)


def convolve(strip, half, mixed, gated, conv, back):
    for d in range(STEPS):
        o = PAIR * d
        weights = jnp.concatenate(
            [strip[half, :, o + 128 : o + 384], strip[half, :, o : o + 256]], axis=0
        )
        skip = MEMBERS * d
        y = dot(mixed[0 : ROWS - skip, :], weights)
        m = dot_rows(gated[skip:ROWS, :], weights)
        if d == 0:
            conv[...] = y
            back[...] = m
        else:
            conv[skip:ROWS, :] += y
            back[0 : ROWS - skip, :] += m


def lag(mixed, gated, half, flipped, outer, lags):
    row = lax.broadcasted_iota(jnp.int32, (PAIR, PAIR), 0)
    column = lax.broadcasted_iota(jnp.int32, (PAIR, PAIR), 1)
    eye = jnp.where(row == column, 1.0, 0.0).astype(BF16)
    flipped[...] = dot_rows(eye, mixed[...]).astype(BF16)
    outer[:, SEQ * BLOCK :] = jnp.zeros((PAIR, 256), F32)
    gated[ROWS:, :] = jnp.zeros((ROWS, PAIR), BF16)
    for d in range(STEPS):
        depth = ROWS if d < STEPS // 2 else ROWS // 2
        skip = MEMBERS * d
        outer[:, PAIR * d : PAIR * d + PAIR] = dot(
            flipped[:, :depth], gated[skip : skip + depth, :]
        )
    wide = 1024 + 128

    def chunk(n, carry):
        base = pl.multiple_of(1024 * n, 128)
        after = pl.multiple_of(base + 128, 128)

        def part(q):
            first = outer[8 * q : 8 * q + 8, pl.ds(base, wide)]
            return first + outer[128 + 8 * q : 136 + 8 * q, pl.ds(after, wide)]

        total = part(0)
        for q in range(1, 16):
            total = total + pltpu.roll(part(q), wide - 8 * q, 1)
        for step in (4, 2, 1):
            total = total + pltpu.roll(pltpu.roll(total, wide - step, 1), 8 - step, 0)
        for k in range(8):
            lags[half, 8 * n + k] = total[0:1, 128 * k : 128 * k + 128]
        return carry

    lax.fori_loop(0, SEQ * BLOCK // 1024, chunk, 0)


def kernel(
    grad_hbm, query_hbm, key_hbm, value_hbm, filter_hbm,
    out_hbm, lag_out,
    grad, query, key, value, taps_in, out,
    mixed_rows, gated_rows, turned, taps_turned,
    taps_send, taps_recv, taps,
    send, recv, strip, mixed, gated, conv, back, flipped, outer,
    back_send, back_recv, lags, lag_recv,
    load_sem, store_sem, own_sem,
    taps_ssem, taps_rsem, send_sem, recv_sem, back_ssem, back_rsem, lag_ssem, lag_rsem,
):
    seq = lax.axis_index("seq")
    ch = lax.axis_index("ch")
    me = seq * CH + ch

    loads = [
        pltpu.make_async_copy(src, dst, load_sem.at[k])
        for k, (src, dst) in enumerate(
            ((key_hbm, key), (value_hbm, value), (grad_hbm, grad), (query_hbm, query), (filter_hbm, taps_in))
        )
    ]
    for load in loads:
        load.start()

    def remote(src, dst, ssem, rsem, target):
        return pltpu.make_async_remote_copy(
            src_ref=src,
            dst_ref=dst,
            send_sem=ssem,
            recv_sem=rsem,
            device_id=target,
            device_id_type=pl.DeviceIdType.LOGICAL,
        )

    barrier = pltpu.get_barrier_semaphore()

    def greet(k, carry):
        pl.semaphore_signal(
            barrier, inc=1, device_id=me ^ (255 - k), device_id_type=pl.DeviceIdType.LOGICAL
        )
        return carry

    lax.fori_loop(0, DEVICES - 1, greet, 0, unroll=5)

    loads[0].wait()
    loads[1].wait()
    products(key, value, mixed_rows)
    loads[2].wait()
    loads[3].wait()
    products(grad, query, gated_rows)
    for tile in range(TILES):
        spread(mixed_rows, gated_rows, tile, turned, send)
    loads[4].wait()
    for half in range(2):
        lanes = pl.ds(pl.multiple_of(256 * half + 128 * (ch // 2), 128), 128)
        taps_turned[...] = taps_in[:, lanes].astype(F32).T
        picked = taps_turned[pl.ds(pl.multiple_of(64 * (ch % 2), 64), 64), :]
        taps_send[:, half, :] = picked.astype(BF16)

    pl.semaphore_wait(barrier, DEVICES - 1)

    pltpu.make_async_copy(taps_send.at[seq], taps_recv.at[seq], taps_rsem).start()

    def send_taps(k, carry):
        other = seq ^ (k + 1)
        remote(taps_send.at[other], taps_recv.at[seq], taps_ssem, taps_rsem, other * CH + ch).start()
        return carry

    lax.fori_loop(0, SEQ - 1, send_taps, 0, unroll=3)

    def exchange(src, dst, ssem, rsem):
        pltpu.make_async_copy(src.at[ch, seq], dst.at[ch, seq], rsem).start()

        def step(k, carry):
            other_seq = seq ^ ((k + 1) // CH)
            other_ch = ch ^ ((k + 1) % CH)
            target = other_seq * CH + other_ch
            remote(src.at[other_ch, other_seq], dst.at[ch, seq], ssem, rsem, target).start()
            return carry

        lax.fori_loop(0, DEVICES - 1, step, 0, unroll=5)

    for half in range(2):
        exchange(send.at[half], recv.at[half], send_sem.at[half], recv_sem.at[half])

    pltpu.make_async_copy(taps_recv, taps_recv, taps_rsem).wait()
    for half in range(2):
        taps[half] = taps_recv[:, half, :].astype(F32)
        toeplitz(taps, half, strip)

    for half in range(2):
        pltpu.make_async_copy(recv.at[half], recv.at[half], recv_sem.at[half]).wait()
        unpack(recv, half, mixed, gated)
        convolve(strip, half, mixed, gated, conv, back)
        pack(conv, back, half, back_send)
        exchange(back_send.at[half], back_recv.at[half], back_ssem.at[half], back_rsem.at[half])
        lag(mixed, gated, half, flipped, outer, lags)
        lag_ch = 2 * half + ch // 2
        lag_slot = lag_recv.at[ch % 2, seq]

        @pl.when(lag_ch == ch)
        def _():
            pltpu.make_async_copy(lags.at[half, seq], lag_slot, lag_rsem).start()

        @pl.when(lag_ch != ch)
        def _():
            remote(lags.at[half, seq], lag_slot, lag_ssem, lag_rsem, seq * CH + lag_ch).start()

        def send_lags(k, carry):
            other = seq ^ (k + 1)
            remote(lags.at[half, other], lag_slot, lag_ssem, lag_rsem, other * CH + lag_ch).start()
            return carry

        lax.fori_loop(0, SEQ - 1, send_lags, 0, unroll=3)

    stores = []
    for half in range(2):
        pltpu.make_async_copy(back_recv.at[half], back_recv.at[half], back_rsem.at[half]).wait()
        for tile in (2 * half, 2 * half + 1):
            collect(back_recv, tile, turned, mixed_rows, gated_rows)
            gradients(tile, mixed_rows, gated_rows, grad, key, value, out)
            lanes = pl.ds(128 * tile, 128)
            store = pltpu.make_async_copy(
                out.at[:, :, :, lanes], out_hbm.at[:, :, :, lanes], store_sem.at[tile]
            )
            store.start()
            stores.append(store)

    pltpu.make_async_copy(lag_recv, lag_recv, lag_rsem).wait()
    lag_out[...] = lag_recv[...].reshape(128, BLOCK).T * SCALE

    pltpu.make_async_copy(
        taps_send.at[pl.ds(0, SEQ - 1)], taps_send.at[pl.ds(0, SEQ - 1)], taps_ssem
    ).wait()
    for half in range(2):
        for buffer, sem in ((send, send_sem), (back_send, back_ssem)):
            for c in range(CH):
                piece = buffer.at[half, c, pl.ds(0, SEQ if c else SEQ - 1)]
                pltpu.make_async_copy(piece, piece, sem.at[half]).wait()

        sent = lags.at[half, pl.ds(0, SEQ - 1)]
        pltpu.make_async_copy(sent, sent, lag_ssem).wait()

        @pl.when(2 * half + ch // 2 != ch)
        def _():
            pltpu.make_async_copy(lags.at[half, 0], lags.at[half, 0], lag_ssem).wait()

    for store in stores:
        store.wait()


def local(grad_output, query_act, key_act, value_act, long_filter):
    vmem = pltpu.VMEM
    dma = pltpu.SemaphoreType.DMA
    message = (2, CH, SEQ, 8, BLOCK)
    return pl.pallas_call(
        kernel,
        out_shape=(
            jax.ShapeDtypeStruct((3, BLOCK, OWN, GROUPS), BF16),
            jax.ShapeDtypeStruct((BLOCK, 128), F32),
        ),
        in_specs=[pl.BlockSpec(memory_space=pl.ANY)] * 5,
        out_specs=[pl.BlockSpec(memory_space=pl.ANY), pl.BlockSpec(memory_space=pltpu.VMEM)],
        scratch_shapes=[
            vmem((BLOCK, OWN, GROUPS), BF16),
            vmem((BLOCK, OWN, GROUPS), BF16),
            vmem((BLOCK, OWN, GROUPS), BF16),
            vmem((BLOCK, OWN, GROUPS), BF16),
            vmem((BLOCK, GROUPS), BF16),
            vmem((3, BLOCK, OWN, GROUPS), BF16),
            vmem((TILES, BLOCK * OWN, 128), F32),
            vmem((TILES, BLOCK * OWN, 128), F32),
            vmem((1024, BLOCK), F32),
            vmem((128, BLOCK), F32),
            vmem((SEQ, 2, BLOCK), BF16),
            vmem((SEQ, 2, BLOCK), BF16),
            vmem((2, SEQ, BLOCK), F32),
            vmem(message, BF16),
            vmem(message, BF16),
            vmem((2, 128, SEQ * BLOCK + 128), BF16),
            vmem((ROWS, PAIR), BF16),
            vmem((2 * ROWS, PAIR), BF16),
            vmem((ROWS, PAIR), F32),
            vmem((ROWS, PAIR), F32),
            vmem((PAIR, ROWS), BF16),
            vmem((PAIR, SEQ * BLOCK + 256), F32),
            vmem(message, BF16),
            vmem(message, BF16),
            vmem((2, SEQ, 1, BLOCK), F32),
            vmem((2, SEQ, 1, BLOCK), F32),
            dma((5,)),
            dma((TILES,)),
            dma,
            dma,
            dma,
            dma((2,)),
            dma((2,)),
            dma((2,)),
            dma((2,)),
            dma,
            dma,
        ],
        compiler_params=pltpu.CompilerParams(
            collective_id=0, has_side_effects=True, vmem_limit_bytes=56 * 2**20
        ),
        cost_estimate=pl.CostEstimate(
            flops=10_000_000_000, bytes_accessed=4_000_000, transcendentals=0
        ),
    )(grad_output, query_act, key_act, value_act, long_filter)


def solution(mesh):
    wide = P("seq", "ch", None)
    in_specs = (wide, wide, wide, wide, P("seq", None))
    out_specs = (P(None, "seq", "ch", None), P("seq", "ch"))
    return jax.shard_map(local, mesh=mesh, in_specs=in_specs, out_specs=out_specs, check_vma=False)
```

time: 722 us -> 73.7 us (0.10); the launches traced: 713 us -> 73.6 us
  waiting for transfers between devices: 418 us -> 0 us
  local copies, waits for them, and re-layouts: 94 us -> 3.76 us
  Pallas kernels: 0 us -> 69.2 us
  blocking collectives: 63.5 us -> 0 us
  matrix products: 61.2 us -> 0 us
  starting transfers between devices: 47.5 us -> 0 us
  between operations: 14.7 us -> 0.65 us
  other arithmetic: 13.6 us -> 0 us
    all_to_all x5 -> x0, waiting for transfers between devices: 393 us -> none  [the longest x1 96.5 us: local(): lax.all_to_all(real_part, 'seq', split_axis=2, concat_axis=1, tiled=True)]
    pallas_call x0 -> x1, Pallas kernels: none -> 69.2 us  [local(): pl.pallas_call(kernel, out_shape=(jax.ShapeDtypeStruct((3, BLOCK, OWN, GR...]
    all_to_all x1 -> x0, blocking collectives: 63.5 us -> none  [local(): lax.all_to_all(result, 'seq', split_axis=1, concat_axis=2, tiled=True)]
    dot_general x12 -> x0, matrix products: 61.2 us -> none  [the longest x8 43.2 us: contract(): return jnp.einsum('bn,janc->jabc', matrix, values, precision=highest)]
    all_to_all x5 -> x0, starting transfers between devices: 47.5 us -> none  [the longest x1 13.5 us: local(): lax.all_to_all(stacked.reshape(1, seq_count, piece_len, width), 'seq', sp...]
    another operation x4 -> x0, local copies, waits for them, and re-layouts: 29.3 us -> none
    reduce_scatter x1 -> x0, waiting for transfers between devices: 25.3 us -> none  [local(): lax.psum_scatter(lag_term, 'ch', scatter_dimension=1, tiled=True)]
    all_to_all x4 -> x0, local copies, waits for them, and re-layouts: 23.4 us -> none  [the longest x1 6.94 us: local(): lax.all_to_all(imag_part, 'seq', split_axis=1, concat_axis=2, tiled=True)]
  transfers between devices with their start and end apart: 6 -> 0, of which waited for: 6 -> 0; matrix products, arithmetic and copies ran while one was open for 9% -> 0% of each run, Pallas kernels for 0% -> 0%
where the time goes in v1:
time: 73.7 us; the launch traced here: 73.6 us
  Pallas kernels  69.2 us (94%)
  local copies, waits for them, and re-layouts  3.76 us (5%)
    pallas_call x1, Pallas kernels, local(): pl.pallas_call(kernel, out_shape=(jax.ShapeDtypeStruct((3, BLOCK, OWN, GR...  69.2 us
    unnamed x4, local copies, waits for them, and re-layouts  3.76 us

profile of v1, /device:TPU:1, one launch (start us, length us, event | category | flops | bytes accessed | tf_op | source)
XLA Modules:
  0.0 73.6 jit_solution(16371844583197758611)
XLA Ops:
  0.6 69.2 %shard_map.68 = (bf16[3,128,4,512]{3,2,1,0:T(4,128)(2,1)}, f32[128,128]{1,0:T(8,128)}) custom-call(bf16[128,4,512]{2,1,0:T(4,128)(2,1)} %grad_hbm.1, bf16[128,4,512]{2,1,0:T(4,128)(2,1)} %query_hbm.1, bf16[128,4,512]{2,1,0:T(4,128)(2,1)} %key_hbm.1, bf16[128,4,512]{2,1,0:T(4,128)(2,1)} %value_hbm.1, bf16[128,512]{1,0:T(8,128)(2,1)} %filter_hbm.1), custom_call_target="tpu_custom_call" | custom-call | flops 10000000000 | bytes 4000000 | tf_op jit(solution)/shard_map/pallas_call | solution.py:340
  69.8 0.0 copy-start
  69.8 3.1 %copy.9 = bf16[3,128,4,512]{3,2,1,0:T(4,128)(2,1)} copy(bf16[3,128,4,512]{3,2,1,0:T(4,128)(2,1)} %get-tuple-element.4) | data formatting | bytes 3145728
  73.0 0.0 copy-done
  73.0 0.6 copy.10
Async XLA Ops:
  69.8 3.1 %copy-start = (f32[128,128]{1,0:T(8,128)S(1)}, f32[128,128]{1,0:T(8,128)}, u32[]{:S(2)}) copy-start(f32[128,128]{1,0:T(8,128)} %get-tuple-element.5) | copy-start | bytes 196612

commit v2 on v1

--- a/solution.py
+++ b/solution.py
@@ -34,8 +34,9 @@
     return jnp.dot(left, right, preferred_element_type=F32)
 
 
-def products(left, right, rows):
+def products(left, right, rows, beside):
     def body(k, carry):
+        beside(k)
         at = pl.ds(pl.multiple_of(16 * k, 16), 16)
         value = (left[at].astype(F32) * right[at].astype(F32)).astype(BF16).astype(F32)
         value = value.reshape(64, GROUPS)
@@ -182,15 +183,22 @@
     lax.fori_loop(0, SEQ * BLOCK // 1024, chunk, 0)
 
 
+def partner(k, seq, ch):
+    turn = (k >> 3) & 7
+    z = ((seq >> 1) + ((turn + 1) >> 1) * (2 * (turn & 1) - 1)) & 7
+    x = ((seq >> 4) + (k >> 6)) & 3
+    return (x << 4) | (z << 1) | ((seq ^ (k >> 2)) & 1), ch ^ (k & 3)
+
+
 def kernel(
     grad_hbm, query_hbm, key_hbm, value_hbm, filter_hbm,
-    out_hbm, lag_out,
-    grad, query, key, value, taps_in, out,
+    out, lag_out,
+    grad, query, key, value, taps_in,
     mixed_rows, gated_rows, turned, taps_turned,
     taps_send, taps_recv, taps,
     send, recv, strip, mixed, gated, conv, back, flipped, outer,
     back_send, back_recv, lags, lag_recv,
-    load_sem, store_sem, own_sem,
+    load_sem,
     taps_ssem, taps_rsem, send_sem, recv_sem, back_ssem, back_rsem, lag_ssem, lag_rsem,
 ):
     seq = lax.axis_index("seq")
@@ -218,28 +226,41 @@
 
     barrier = pltpu.get_barrier_semaphore()
 
-    def greet(k, carry):
-        pl.semaphore_signal(
-            barrier, inc=1, device_id=me ^ (255 - k), device_id_type=pl.DeviceIdType.LOGICAL
-        )
-        return carry
-
-    lax.fori_loop(0, DEVICES - 1, greet, 0, unroll=5)
-
+    def greet(first, count):
+        def signal(n):
+            pl.semaphore_signal(
+                barrier,
+                inc=1,
+                device_id=me ^ (first - n),
+                device_id_type=pl.DeviceIdType.LOGICAL,
+            )
+
+        if isinstance(first, int):
+
+            def body(n, carry):
+                signal(n)
+                return carry
+
+            lax.fori_loop(0, count, body, 0, unroll=5)
+        else:
+            for n in range(count):
+                signal(n)
+
+    greet(255, 255)
     loads[0].wait()
     loads[1].wait()
-    products(key, value, mixed_rows)
+    products(key, value, mixed_rows, lambda k: None)
     loads[2].wait()
     loads[3].wait()
-    products(grad, query, gated_rows)
-    for tile in range(TILES):
-        spread(mixed_rows, gated_rows, tile, turned, send)
+    products(grad, query, gated_rows, lambda k: None)
     loads[4].wait()
     for half in range(2):
         lanes = pl.ds(pl.multiple_of(256 * half + 128 * (ch // 2), 128), 128)
         taps_turned[...] = taps_in[:, lanes].astype(F32).T
         picked = taps_turned[pl.ds(pl.multiple_of(64 * (ch % 2), 64), 64), :]
         taps_send[:, half, :] = picked.astype(BF16)
+    for tile in (0, 1):
+        spread(mixed_rows, gated_rows, tile, turned, send)
 
     pl.semaphore_wait(barrier, DEVICES - 1)
 
@@ -256,16 +277,17 @@
         pltpu.make_async_copy(src.at[ch, seq], dst.at[ch, seq], rsem).start()
 
         def step(k, carry):
-            other_seq = seq ^ ((k + 1) // CH)
-            other_ch = ch ^ ((k + 1) % CH)
+            other_seq, other_ch = partner(k + 1, seq, ch)
             target = other_seq * CH + other_ch
             remote(src.at[other_ch, other_seq], dst.at[ch, seq], ssem, rsem, target).start()
             return carry
 
         lax.fori_loop(0, DEVICES - 1, step, 0, unroll=5)
 
-    for half in range(2):
-        exchange(send.at[half], recv.at[half], send_sem.at[half], recv_sem.at[half])
+    exchange(send.at[0], recv.at[0], send_sem.at[0], recv_sem.at[0])
+    for tile in (2, 3):
+        spread(mixed_rows, gated_rows, tile, turned, send)
+    exchange(send.at[1], recv.at[1], send_sem.at[1], recv_sem.at[1])
 
     pltpu.make_async_copy(taps_recv, taps_recv, taps_rsem).wait()
     for half in range(2):
@@ -297,18 +319,11 @@
 
         lax.fori_loop(0, SEQ - 1, send_lags, 0, unroll=3)
 
-    stores = []
     for half in range(2):
         pltpu.make_async_copy(back_recv.at[half], back_recv.at[half], back_rsem.at[half]).wait()
         for tile in (2 * half, 2 * half + 1):
             collect(back_recv, tile, turned, mixed_rows, gated_rows)
             gradients(tile, mixed_rows, gated_rows, grad, key, value, out)
-            lanes = pl.ds(128 * tile, 128)
-            store = pltpu.make_async_copy(
-                out.at[:, :, :, lanes], out_hbm.at[:, :, :, lanes], store_sem.at[tile]
-            )
-            store.start()
-            stores.append(store)
 
     pltpu.make_async_copy(lag_recv, lag_recv, lag_rsem).wait()
     lag_out[...] = lag_recv[...].reshape(128, BLOCK).T * SCALE
@@ -329,29 +344,38 @@
         def _():
             pltpu.make_async_copy(lags.at[half, 0], lags.at[half, 0], lag_ssem).wait()
 
-    for store in stores:
-        store.wait()
+
+def hand_over(out, lags, out_final, lag_final, sem):
+    copies = [
+        pltpu.make_async_copy(out.at[k, pl.ds(64 * h, 64)], out_final.at[k, pl.ds(64 * h, 64)], sem.at[2 * k + h])
+        for k in range(3)
+        for h in range(2)
+    ]
+    copies.append(pltpu.make_async_copy(lags, lag_final, sem.at[6]))
+    for copy in copies:
+        copy.start()
+    for copy in copies:
+        copy.wait()
 
 
 def local(grad_output, query_act, key_act, value_act, long_filter):
     vmem = pltpu.VMEM
     dma = pltpu.SemaphoreType.DMA
     message = (2, CH, SEQ, 8, BLOCK)
-    return pl.pallas_call(
+    out, lags = pl.pallas_call(
         kernel,
         out_shape=(
-            jax.ShapeDtypeStruct((3, BLOCK, OWN, GROUPS), BF16),
-            jax.ShapeDtypeStruct((BLOCK, 128), F32),
+            pltpu.VMEM((3, BLOCK, OWN, GROUPS), BF16),
+            pltpu.VMEM((BLOCK, 128), F32),
         ),
-        in_specs=[pl.BlockSpec(memory_space=pl.ANY)] * 5,
-        out_specs=[pl.BlockSpec(memory_space=pl.ANY), pl.BlockSpec(memory_space=pltpu.VMEM)],
+        in_specs=[pl.BlockSpec(memory_space=pltpu.HBM)] * 5,
+        out_specs=[pl.BlockSpec(memory_space=pltpu.VMEM)] * 2,
         scratch_shapes=[
             vmem((BLOCK, OWN, GROUPS), BF16),
             vmem((BLOCK, OWN, GROUPS), BF16),
             vmem((BLOCK, OWN, GROUPS), BF16),
             vmem((BLOCK, OWN, GROUPS), BF16),
             vmem((BLOCK, GROUPS), BF16),
-            vmem((3, BLOCK, OWN, GROUPS), BF16),
             vmem((TILES, BLOCK * OWN, 128), F32),
             vmem((TILES, BLOCK * OWN, 128), F32),
             vmem((1024, BLOCK), F32),
@@ -373,8 +397,6 @@
             vmem((2, SEQ, 1, BLOCK), F32),
             vmem((2, SEQ, 1, BLOCK), F32),
             dma((5,)),
-            dma((TILES,)),
-            dma,
             dma,
             dma,
             dma((2,)),
@@ -391,6 +413,7 @@
             flops=10_000_000_000, bytes_accessed=4_000_000, transcendentals=0
         ),
     )(grad_output, query_act, key_act, value_act, long_filter)
+    return out, lags
 
 
 def solution(mesh):

time: 73.7 us -> 68.5 us (0.929)
  Pallas kernels: 69.2 us -> 66 us
  local copies, waits for them, and re-layouts: 3.76 us -> 1.77 us
    pallas_call x1, Pallas kernels: 69.2 us -> 66 us  [local(): pl.pallas_call(kernel, out_shape=(pltpu.VMEM((3, BLOCK, OWN, GROUPS), BF1...]
    unnamed x4 -> x2, local copies, waits for them, and re-layouts: 3.76 us -> 1.77 us
where the time goes in v2:
time: 68.5 us
  Pallas kernels  66 us (96%)
  local copies, waits for them, and re-layouts  1.77 us (3%)
    pallas_call x1, Pallas kernels, local(): pl.pallas_call(kernel, out_shape=(pltpu.VMEM((3, BLOCK, OWN, GROUPS), BF1...  66 us
    unnamed x2, local copies, waits for them, and re-layouts  1.77 us

profile of v2, /device:TPU:1, one launch (start us, length us, event | category | flops | bytes accessed | tf_op | source)
XLA Modules:
  0.0 68.5 jit_solution(5592839825010021445)
XLA Ops:
  0.6 66.0 %shard_map.68 = (bf16[3,128,4,512]{3,2,1,0:T(4,128)(2,1)S(1)}, f32[128,128]{1,0:T(8,128)S(1)}) custom-call(bf16[128,4,512]{2,1,0:T(4,128)(2,1)} %grad_hbm.1, bf16[128,4,512]{2,1,0:T(4,128)(2,1)} %query_hbm.1, bf16[128,4,512]{2,1,0:T(4,128)(2,1)} %key_hbm.1, bf16[128,4,512]{2,1,0:T(4,128)(2,1)} %value_hbm.1, bf16[128,512]{1,0:T(8,128)(2,1)} %filter_hbm.1), custom_call_target="tpu_custom_call" | custom-call | flops 10000000000 | bytes 4000000 | tf_op jit(solution)/shard_map/pallas_call | solution.py:365
  66.7 1.1 %copy.9 = bf16[3,128,4,512]{3,2,1,0:T(4,128)(2,1)} copy(bf16[3,128,4,512]{3,2,1,0:T(4,128)(2,1)S(1)} %get-tuple-element.2) | data formatting | bytes 3145728
  67.8 0.6 copy.10

commit v3 on v2

--- a/solution.py
+++ b/solution.py
@@ -184,9 +184,11 @@
 
 
 def partner(k, seq, ch):
-    turn = (k >> 3) & 7
+    k = (k + 248) & 255
+    turn = 7 - ((k >> 3) & 7)
     z = ((seq >> 1) + ((turn + 1) >> 1) * (2 * (turn & 1) - 1)) & 7
-    x = ((seq >> 4) + (k >> 6)) & 3
+    far = k >> 6
+    x = ((seq >> 4) + 2 - far - (far >> 1) - 2 * ((far >> 1) & far)) & 3
     return (x << 4) | (z << 1) | ((seq ^ (k >> 2)) & 1), ch ^ (k & 3)
 
 
@@ -241,7 +243,7 @@
                 signal(n)
                 return carry
 
-            lax.fori_loop(0, count, body, 0, unroll=5)
+            lax.fori_loop(0, count, body, 0, unroll=51)
         else:
             for n in range(count):
                 signal(n)
@@ -282,7 +284,7 @@
             remote(src.at[other_ch, other_seq], dst.at[ch, seq], ssem, rsem, target).start()
             return carry
 
-        lax.fori_loop(0, DEVICES - 1, step, 0, unroll=5)
+        lax.fori_loop(0, DEVICES - 1, step, 0, unroll=17)
 
     exchange(send.at[0], recv.at[0], send_sem.at[0], recv_sem.at[0])
     for tile in (2, 3):

time: 68.5 us -> 67.2 us (0.981)
  Pallas kernels: 66 us -> 64.7 us
    pallas_call x1, Pallas kernels: 66 us -> 64.7 us  [local(): pl.pallas_call(kernel, out_shape=(pltpu.VMEM((3, BLOCK, OWN, GROUPS), BF1...]
where the time goes in v3:
time: 67.2 us; the launch traced here: 67.1 us
  Pallas kernels  64.7 us (96%)
  local copies, waits for them, and re-layouts  1.77 us (3%)
    pallas_call x1, Pallas kernels, local(): pl.pallas_call(kernel, out_shape=(pltpu.VMEM((3, BLOCK, OWN, GROUPS), BF1...  64.7 us
    unnamed x2, local copies, waits for them, and re-layouts  1.77 us

profile of v3, /device:TPU:1, one launch (start us, length us, event | category | flops | bytes accessed | tf_op | source)
XLA Modules:
  0.0 67.1 jit_solution(4189081452402497028)
XLA Ops:
  0.6 64.7 %shard_map.68 = (bf16[3,128,4,512]{3,2,1,0:T(4,128)(2,1)S(1)}, f32[128,128]{1,0:T(8,128)S(1)}) custom-call(bf16[128,4,512]{2,1,0:T(4,128)(2,1)} %grad_hbm.1, bf16[128,4,512]{2,1,0:T(4,128)(2,1)} %query_hbm.1, bf16[128,4,512]{2,1,0:T(4,128)(2,1)} %key_hbm.1, bf16[128,4,512]{2,1,0:T(4,128)(2,1)} %value_hbm.1, bf16[128,512]{1,0:T(8,128)(2,1)} %filter_hbm.1), custom_call_target="tpu_custom_call" | custom-call | flops 10000000000 | bytes 4000000 | tf_op jit(solution)/shard_map/pallas_call | solution.py:367
  65.4 1.1 %copy.9 = bf16[3,128,4,512]{3,2,1,0:T(4,128)(2,1)} copy(bf16[3,128,4,512]{3,2,1,0:T(4,128)(2,1)S(1)} %get-tuple-element.2) | data formatting | bytes 3145728
  66.5 0.6 copy.10

commit v4 on v3

--- a/solution.py
+++ b/solution.py
@@ -34,16 +34,16 @@
     return jnp.dot(left, right, preferred_element_type=F32)
 
 
-def products(left, right, rows, beside):
+def products(left, right, half, rows):
+    lanes = slice(256 * half, 256 * half + 256)
+
     def body(k, carry):
-        beside(k)
         at = pl.ds(pl.multiple_of(16 * k, 16), 16)
-        value = (left[at].astype(F32) * right[at].astype(F32)).astype(BF16).astype(F32)
-        value = value.reshape(64, GROUPS)
-        for tile in range(TILES):
-            rows[tile, pl.ds(pl.multiple_of(64 * k, 64), 64), :] = value[
-                :, 128 * tile : 128 * tile + 128
-            ]
+        value = left[at, :, lanes].astype(F32) * right[at, :, lanes].astype(F32)
+        value = value.astype(BF16).astype(F32).reshape(64, 256)
+        at = pl.ds(pl.multiple_of(64 * k, 64), 64)
+        rows[2 * half, at, :] = value[:, :128]
+        rows[2 * half + 1, at, :] = value[:, 128:]
         return carry
 
     lax.fori_loop(0, BLOCK // 16, body, 0)
@@ -180,7 +180,7 @@
             lags[half, 8 * n + k] = total[0:1, 128 * k : 128 * k + 128]
         return carry
 
-    lax.fori_loop(0, SEQ * BLOCK // 1024, chunk, 0)
+    lax.fori_loop(0, SEQ * BLOCK // 1024, chunk, 0, unroll=4)
 
 
 def partner(k, seq, ch):
@@ -228,33 +228,23 @@
 
     barrier = pltpu.get_barrier_semaphore()
 
-    def greet(first, count):
-        def signal(n):
-            pl.semaphore_signal(
-                barrier,
-                inc=1,
-                device_id=me ^ (first - n),
-                device_id_type=pl.DeviceIdType.LOGICAL,
-            )
-
-        if isinstance(first, int):
-
-            def body(n, carry):
-                signal(n)
-                return carry
-
-            lax.fori_loop(0, count, body, 0, unroll=51)
-        else:
-            for n in range(count):
-                signal(n)
-
-    greet(255, 255)
+    far = 0b10100111
+
+    def greet(k, carry):
+        pl.semaphore_signal(
+            barrier, inc=1, device_id=me ^ far ^ k, device_id_type=pl.DeviceIdType.LOGICAL
+        )
+        return carry
+
+    lax.fori_loop(0, far, greet, 0, unroll=167)
+    lax.fori_loop(far + 1, DEVICES, greet, 0, unroll=44)
+
     loads[0].wait()
     loads[1].wait()
-    products(key, value, mixed_rows, lambda k: None)
+    products(key, value, 0, mixed_rows)
     loads[2].wait()
     loads[3].wait()
-    products(grad, query, gated_rows, lambda k: None)
+    products(grad, query, 0, gated_rows)
     loads[4].wait()
     for half in range(2):
         lanes = pl.ds(pl.multiple_of(256 * half + 128 * (ch // 2), 128), 128)
@@ -273,7 +263,7 @@
         remote(taps_send.at[other], taps_recv.at[seq], taps_ssem, taps_rsem, other * CH + ch).start()
         return carry
 
-    lax.fori_loop(0, SEQ - 1, send_taps, 0, unroll=3)
+    lax.fori_loop(0, SEQ - 1, send_taps, 0, unroll=21)
 
     def exchange(src, dst, ssem, rsem):
         pltpu.make_async_copy(src.at[ch, seq], dst.at[ch, seq], rsem).start()
@@ -287,6 +277,8 @@
         lax.fori_loop(0, DEVICES - 1, step, 0, unroll=17)
 
     exchange(send.at[0], recv.at[0], send_sem.at[0], recv_sem.at[0])
+    products(key, value, 1, mixed_rows)
+    products(grad, query, 1, gated_rows)
     for tile in (2, 3):
         spread(mixed_rows, gated_rows, tile, turned, send)
     exchange(send.at[1], recv.at[1], send_sem.at[1], recv_sem.at[1])
@@ -319,7 +311,7 @@
             remote(lags.at[half, other], lag_slot, lag_ssem, lag_rsem, other * CH + lag_ch).start()
             return carry
 
-        lax.fori_loop(0, SEQ - 1, send_lags, 0, unroll=3)
+        lax.fori_loop(0, SEQ - 1, send_lags, 0, unroll=21)
 
     for half in range(2):
         pltpu.make_async_copy(back_recv.at[half], back_recv.at[half], back_rsem.at[half]).wait()

time: 67.2 us -> 66.7 us (level)
  no operation moved by 1% of the time
where the time goes in v4:
time: 66.7 us; the launch traced here: 66.5 us
  Pallas kernels  64.1 us (96%)
  local copies, waits for them, and re-layouts  1.77 us (3%)
    pallas_call x1, Pallas kernels, local(): pl.pallas_call(kernel, out_shape=(pltpu.VMEM((3, BLOCK, OWN, GROUPS), BF1...  64.1 us
    unnamed x2, local copies, waits for them, and re-layouts  1.77 us

profile of v4, /device:TPU:1, one launch (start us, length us, event | category | flops | bytes accessed | tf_op | source)
XLA Modules:
  0.0 66.5 jit_solution(14635979470777203348)
XLA Ops:
  0.6 64.1 %shard_map.68 = (bf16[3,128,4,512]{3,2,1,0:T(4,128)(2,1)S(1)}, f32[128,128]{1,0:T(8,128)S(1)}) custom-call(bf16[128,4,512]{2,1,0:T(4,128)(2,1)} %grad_hbm.1, bf16[128,4,512]{2,1,0:T(4,128)(2,1)} %query_hbm.1, bf16[128,4,512]{2,1,0:T(4,128)(2,1)} %key_hbm.1, bf16[128,4,512]{2,1,0:T(4,128)(2,1)} %value_hbm.1, bf16[128,512]{1,0:T(8,128)(2,1)} %filter_hbm.1), custom_call_target="tpu_custom_call" | custom-call | flops 10000000000 | bytes 4000000 | tf_op jit(solution)/shard_map/pallas_call | solution.py:359
  64.8 1.1 %copy.9 = bf16[3,128,4,512]{3,2,1,0:T(4,128)(2,1)} copy(bf16[3,128,4,512]{3,2,1,0:T(4,128)(2,1)S(1)} %get-tuple-element.2) | data formatting | bytes 3145728
  65.9 0.6 copy.10

commit v5 on v4

--- a/solution.py
+++ b/solution.py
@@ -274,7 +274,7 @@
             remote(src.at[other_ch, other_seq], dst.at[ch, seq], ssem, rsem, target).start()
             return carry
 
-        lax.fori_loop(0, DEVICES - 1, step, 0, unroll=17)
+        lax.fori_loop(0, DEVICES - 1, step, 0, unroll=51)
 
     exchange(send.at[0], recv.at[0], send_sem.at[0], recv_sem.at[0])
     products(key, value, 1, mixed_rows)

time: 66.7 us -> 66.7 us (level)
  no operation moved by 1% of the time
where the time goes in v5:
time: 66.7 us; the launch traced here: 66.5 us
  Pallas kernels  64.1 us (96%)
  local copies, waits for them, and re-layouts  1.77 us (3%)
    pallas_call x1, Pallas kernels, local(): pl.pallas_call(kernel, out_shape=(pltpu.VMEM((3, BLOCK, OWN, GROUPS), BF1...  64.1 us
    unnamed x2, local copies, waits for them, and re-layouts  1.77 us

profile of v5, /device:TPU:1, one launch (start us, length us, event | category | flops | bytes accessed | tf_op | source)
XLA Modules:
  0.0 66.5 jit_solution(10626461102383863341)
XLA Ops:
  0.6 64.1 %shard_map.68 = (bf16[3,128,4,512]{3,2,1,0:T(4,128)(2,1)S(1)}, f32[128,128]{1,0:T(8,128)S(1)}) custom-call(bf16[128,4,512]{2,1,0:T(4,128)(2,1)} %grad_hbm.1, bf16[128,4,512]{2,1,0:T(4,128)(2,1)} %query_hbm.1, bf16[128,4,512]{2,1,0:T(4,128)(2,1)} %key_hbm.1, bf16[128,4,512]{2,1,0:T(4,128)(2,1)} %value_hbm.1, bf16[128,512]{1,0:T(8,128)(2,1)} %filter_hbm.1), custom_call_target="tpu_custom_call" | custom-call | flops 10000000000 | bytes 4000000 | tf_op jit(solution)/shard_map/pallas_call | solution.py:359
  64.8 1.1 %copy.9 = bf16[3,128,4,512]{3,2,1,0:T(4,128)(2,1)} copy(bf16[3,128,4,512]{3,2,1,0:T(4,128)(2,1)S(1)} %get-tuple-element.2) | data formatting | bytes 3145728
  65.9 0.6 copy.10
